TPU v7x, 32 devices: a whole 2x2x4 slice. The times are simulated.
32 devices in a mesh: dp: 4 (over x, core), frame: 2 (over y), space: 4 (over z).
Axes of the slice: x: 2, y: 2, z: 4, core: 2. Of those that a mesh axis runs over, the one named last changes fastest.
Arguments:
- clip_tokens: bfloat16 [4, 16, 1024, 1024], P('dp', 'frame', 'space'), may hold values from -6 to 6
- lookback: int32 [4], P('dp'), may hold values from 2 to 16
- valid_frames: int32 [4], P('dp'), may hold values from 1 to 16
- spatial_gain: float32 [1024], replicated, may hold values from 0.1 to 1.9
- spatial_qkv: bfloat16 [1024, 3072], P('frame'), may hold values from -1 to 1
- spatial_out: bfloat16 [1024, 1024], P('frame'), may hold values from -0.375 to 0.375
- temporal_gain: float32 [1024], replicated, may hold values from 0.1 to 1.9
- temporal_qkv: bfloat16 [1024, 3072], P('frame'), may hold values from -1 to 1
- temporal_out: bfloat16 [1024, 1024], P('frame'), may hold values from -0.375 to 0.375
- cotangent: bfloat16 [4, 16, 1024, 1024], P('dp', 'frame', 'space'), may hold values from -0.3125 to 0.3125
Outputs:
- block_out: float32 [4, 16, 1024, 1024], P('dp', 'frame', 'space')
- grad_temporal_out: float32 [1024, 1024], P('frame')
All inputs are finite; a program needn't handle non-finite values.
Results may differ from a plain program's by a relative error of at most 0.039.
The roundings to bfloat16 on the way count: a program that leaves them out, or rounds other values in their place, can miss the bound.
Values may be sent and summed in bfloat16 or wider, within the bound.
A program may use at most 448 MiB of HBM per device.

v0:
```python
import jax
import jax.numpy as jnp
from jax import lax
from jax.sharding import PartitionSpec as P

HD = 64


norm_eps = 1e-06
score_scale = 0.125


def rms_norm(row_block, gain):
    values = row_block.astype(jnp.float32)
    mean_square = jnp.mean(values * values, axis=-1, keepdims=True)
    return (values * lax.rsqrt(mean_square + norm_eps) * gain).astype(jnp.bfloat16)


def fold_rows(activations, weight_rows):
    return jnp.dot(activations, weight_rows, preferred_element_type=jnp.float32)


def frame_visible(lookback, valid_frames, frame_total):
    query_pos = lax.broadcasted_iota(jnp.int32, (frame_total, frame_total), 0)[None]
    key_pos = lax.broadcasted_iota(jnp.int32, (frame_total, frame_total), 1)[None]
    reach = lookback[:, None, None]
    live = valid_frames[:, None, None]
    return (
        (key_pos <= query_pos)
        & (query_pos - key_pos < reach)
        & ((key_pos < live) | (key_pos == query_pos))
    )


def temporal_core(query_rows, key_rows, value_rows, visible):
    clips_in, frames_in, patches_in, pairs_in, _ = query_rows.shape
    split_shape = (clips_in, frames_in, patches_in, pairs_in, 2, HD)
    query_split = query_rows.reshape(split_shape)
    key_split = key_rows.reshape(split_shape)
    value_split = value_rows.reshape(split_shape)
    scores = (
        jnp.einsum(
            "ctpjed,cspjed->cpjets", query_split, key_split, preferred_element_type=jnp.float32
        )
        * score_scale
    )
    seen_mask = visible[:, None, None, None, :, :]
    row_best = jnp.max(jnp.where(seen_mask, scores, -1e30), axis=-1, keepdims=True)
    temporal_weights = jnp.where(seen_mask, jnp.exp(scores - row_best), 0.0)
    temporal_sum = jnp.sum(temporal_weights, axis=-1)
    mixed_rows = jnp.einsum(
        "cpjets,cspjed->ctpjed",
        temporal_weights.astype(jnp.bfloat16),
        value_split,
        preferred_element_type=jnp.float32,
    )
    mixed_rows = mixed_rows / jnp.transpose(temporal_sum, (0, 4, 1, 2, 3))[..., None]
    return mixed_rows.astype(jnp.bfloat16).reshape(
        clips_in, frames_in, patches_in, pairs_in, 2 * HD
    )


def on_device(
    clip_tokens,
    lookback,
    valid_frames,
    spatial_gain,
    spatial_qkv,
    spatial_out,
    temporal_gain,
    temporal_qkv,
    temporal_out,
    cotangent,
):
    clip_count, frames_here, patches_here, width = clip_tokens.shape
    group_count = clip_count * frames_here
    total_rows = group_count * patches_here
    head_count = width // HD
    pair_count = head_count // 2
    flat_rows = clip_tokens.reshape(total_rows, width)
    normed = rms_norm(flat_rows, spatial_gain)
    projected = fold_rows(normed, lax.all_gather(spatial_qkv, "frame", axis=0, tiled=True)).astype(
        jnp.bfloat16
    )
    queries = projected[:, :width].reshape(group_count, patches_here, head_count, HD)
    keys_values = projected[:, width:].reshape(group_count, patches_here, 2 * width)
    shard_block = lax.all_gather(keys_values, "space", axis=1, tiled=True)
    row_best = jnp.full((group_count, head_count, patches_here), -1e30, jnp.float32)
    count_here = shard_block.shape[1]
    key_rows = shard_block[:, :, :width].reshape(group_count, count_here, head_count, HD)
    value_rows = shard_block[:, :, width:].reshape(group_count, count_here, head_count, HD)
    scores = (
        jnp.einsum("gqhd,gkhd->ghqk", queries, key_rows, preferred_element_type=jnp.float32)
        * score_scale
    )
    new_best = jnp.maximum(row_best, jnp.max(scores, axis=-1))
    attn_weights = jnp.exp(scores - new_best[..., None])
    weight_sum = jnp.sum(attn_weights, axis=-1)
    update = jnp.einsum(
        "ghqk,gkhd->gqhd",
        attn_weights.astype(jnp.bfloat16),
        value_rows,
        preferred_element_type=jnp.float32,
    )
    accumulated = update
    row_best, weight_sum, accumulated = (new_best, weight_sum, accumulated)
    spatial_attn = (
        (accumulated / jnp.transpose(weight_sum, (0, 2, 1))[..., None])
        .astype(jnp.bfloat16)
        .reshape(total_rows, width)
    )
    spatial_proj = fold_rows(spatial_attn, lax.all_gather(spatial_out, "frame", axis=0, tiled=True))
    after_spatial = flat_rows.astype(jnp.float32) + spatial_proj
    normed_next = rms_norm(after_spatial, temporal_gain)
    visible = frame_visible(lookback, valid_frames, frames_here * lax.axis_size("frame"))

    def split_pairs(column_block, leading):
        return column_block.reshape(leading + (pair_count, 2 * HD))

    patch_tokens = lax.all_to_all(
        normed_next.reshape(clip_count, frames_here, patches_here, width),
        "frame",
        split_axis=2,
        concat_axis=1,
        tiled=True,
    )
    leading = tuple(patch_tokens.shape[:3])
    token_rows = patch_tokens.reshape(-1, width)
    projected_patch = fold_rows(
        token_rows, lax.all_gather(temporal_qkv, "frame", axis=0, tiled=True)
    ).astype(jnp.bfloat16)
    result_rows = temporal_core(
        split_pairs(projected_patch[:, :width], leading),
        split_pairs(projected_patch[:, width : 2 * width], leading),
        split_pairs(projected_patch[:, 2 * width :], leading),
        visible,
    )
    temporal_rows = lax.all_to_all(
        result_rows.reshape(leading + (width,)), "frame", split_axis=1, concat_axis=2, tiled=True
    )
    temporal_attn = temporal_rows.reshape(total_rows, width)
    temporal_proj = fold_rows(
        temporal_attn, lax.all_gather(temporal_out, "frame", axis=0, tiled=True)
    )
    block_out = (after_spatial + temporal_proj).reshape(clip_tokens.shape)
    grad_rows = cotangent.reshape(total_rows, width)
    grad_share = lax.psum_scatter(
        lax.dot_general(
            grad_rows, temporal_attn, (((0,), (0,)), ((), ())), preferred_element_type=jnp.float32
        ).astype(jnp.bfloat16),
        "frame",
        scatter_dimension=0,
        tiled=True,
    )
    grad_out = lax.psum(grad_share, ("dp", "space")).astype(jnp.float32)
    return (block_out, grad_out)


def solution(mesh):
    placed = (
        P("dp", "frame", "space", None),
        P("dp"),
        P("dp"),
        P(),
        P("frame", None),
        P("frame", None),
        P(),
        P("frame", None),
        P("frame", None),
        P("dp", "frame", "space", None),
    )
    return jax.shard_map(
        on_device,
        mesh=mesh,
        in_specs=placed,
        out_specs=(P("dp", "frame", "space", None), P("frame", None)),
        check_vma=False,
    )
```

profile of v0, /device:TPU:0, one launch (start us, length us, event | category | flops | bytes accessed | tf_op | source)
XLA Modules:
  0.0 1364.3 jit_solution(9143355893505909414)
XLA Ops:
  7.2 0.0 all-gather.6.cloned.1.call-start
  7.2 0.7 all-gather.6.cloned.1.call-update
  7.9 0.0 all-gather.8.cloned.1.call-start
  7.9 3.1 fusion.15
  11.0 4.2 fusion.17
  15.2 77.4 %all-gather.6.cloned.1.call-done = bf16[1024,3072]{1,0:T(8,128)(2,1)} async-done(((bf16[512,3072]{1,0:T(8,128)(2,1)}), bf16[1024,3072]{1,0:T(8,128)(2,1)}) %all-gather.6.cloned.1.call-update) | async-done | bytes 6291472 | tf_op jit(solution)/shard_map/all_gather | solution.py:82
  92.7 19.4 %convolution_convert_fusion.1 = bf16[2048,3072]{1,0:T(8,128)(2,1)} fusion(bf16[2048,1024]{1,0:T(8,128)(2,1)} %fusion.17, bf16[1024,3072]{1,0:T(8,128)(2,1)} %all-gather.6.cloned.1.call-done), kind=kOutput, calls=%fused_computation.11 | convolution fusion | flops 12891193344 | bytes 23068672 | tf_op jit(solution)/shard_map/dot_general | solution.py:20
  112.1 8.4 slice.28
  120.5 0.0 all-gather.8.cloned.1.call-update
  120.5 0.0 all-gather.10.cloned.1.call-start
  120.6 0.7 all-gather.10.cloned.1.call-update
  121.3 0.3 all-gather.12.cloned.1.call-start
  121.5 0.3 all-gather.12.cloned.1.call-update
  121.8 4.6 slice.30
  126.4 12.3 reshape.157
  138.7 543.4 %all-gather.8.cloned.1.call-done = bf16[8,1024,2048]{2,1,0:T(8,128)(2,1)} async-done(((bf16[8,256,2048]{2,1,0:T(8,128)(2,1)}), bf16[8,1024,2048]{2,1,0:T(8,128)(2,1)}) %all-gather.8.cloned.1.call-update) | async-done | bytes 33554448 | tf_op jit(solution)/shard_map/all_gather | solution.py:87
  682.1 23.3 %fusion.33 = (bf16[8,1024,1024]{2,1,0:T(8,128)(2,1)}, bf16[8,1024,1024]{2,1,0:T(8,128)(2,1)}) fusion(bf16[8,1024,2048]{2,1,0:T(8,128)(2,1)} %all-gather.8.cloned.1.call-done), kind=kLoop, calls=%fused_computation.50 | loop fusion | bytes 67108864 | tf_op jit(solution)/shard_map/slice | solution.py:91
  705.3 21.9 %copy.112 = bf16[8,1024,1024]{1,2,0:T(8,128)(2,1)} copy(bf16[8,1024,1024]{2,1,0:T(8,128)(2,1)} %get-tuple-element.17) | data formatting | bytes 33554432 | tf_op jit(solution)/shard_map/slice | solution.py:90
  727.2 55.0 %multiply_reduce_fusion = (f32[8,16,256]{2,1,0:T(8,128)S(1)}, f32[8,16,256,1024]{3,2,1,0:T(8,128)}) fusion(bf16[8,1024,16,64]{1,3,2,0:T(8,128)(2,1)} %bitcast.69, bf16[8,256,16,64]{3,2,1,0:T(8,128)(2,1)} %reshape.157), kind=kOutput, calls=%fused_computation.2 | convolution fusion | flops 4362043392 | bytes 155320320 | tf_op jit(solution)/shard_map/gqhd,gkhd->ghqk/dot_general | solution.py:93
  782.3 21.6 %copy.110 = bf16[8,1024,1024]{1,2,0:T(8,128)(2,1)} copy(bf16[8,1024,1024]{2,1,0:T(8,128)(2,1)} %get-tuple-element.16) | data formatting | bytes 33554432 | tf_op jit(solution)/shard_map/slice | solution.py:91
  803.9 41.1 %fusion.1 = f32[8,16,256]{2,1,0:T(8,128)S(1)} fusion(f32[8,16,256,1024]{3,2,1,0:T(8,128)} %get-tuple-element.24, f32[8,16,256]{2,1,0:T(8,128)S(1)} %broadcast_maximum_fusion), kind=kLoop, calls=%fused_computation.3 | loop fusion | flops 100630528 | bytes 134479872 | tf_op jit(solution)/shard_map/reduce_sum | solution.py:98
  845.0 49.9 %fusion.12 = bf16[8,256,16,64]{1,3,2,0:T(8,128)(2,1)} fusion(f32[8,256,16]{1,2,0:T(8,128)S(1)} %bitcast.82, bf16[8,1024,16,64]{1,3,2,0:T(8,128)(2,1)} %bitcast.73, f32[8,16,256,1024]{3,2,1,0:T(8,128)} %get-tuple-element.24, f32[8,16,256]{2,1,0:T(8,128)S(1)} %broadcast_maximum_fusion), kind=kOutput, calls=%fused_computation.17 | convolution fusion | flops 4399824896 | bytes 155451392 | tf_op jit(solution)/shard_map/ghqk,gkhd->gqhd/dot_general | solution.py:99
  894.9 5.1 copy.114
  900.0 3.5 copy.141
  903.5 9.5 multiply_reduce_fusion.1
  912.9 0.0 copy-start
  912.9 3.4 copy-done
  916.3 0.0 copy-done.2
  916.3 1.3 multiply_convert_fusion
  917.7 4.3 copy.115
  922.0 5.6 all-to-all-start
  927.6 0.0 reduce-scatter.2.cloned.1.call-start
  929.0 46.4 %all-to-all-done = bf16[1,8,256,1024]{3,1,0,2:T(8,128)(2,1)} async-done(((bf16[1,8,256,1024]{3,1,0,2:T(8,128)(2,1)}), bf16[1,8,256,1024]{3,1,0,2:T(8,128)(2,1)}, u32[]{:S(2)}, u32[]{:S(2)}) %all-to-all-start) | async-done | bytes 4194336 | tf_op jit(solution)/shard_map/all_to_all | solution.py:120
  975.4 4.5 copy.116
  979.9 2.4 copy.117
  982.3 16.6 %convolution_convert_fusion = bf16[2048,3072]{1,0:T(8,128)(2,1)S(1)} fusion(bf16[2048,1024]{1,0:T(8,128)(2,1)} %bitcast.80, bf16[1024,3072]{1,0:T(8,128)(2,1)} %all-gather.12.cloned.1.call-done), kind=kOutput, calls=%fused_computation.10 | convolution fusion | flops 12891193344 | bytes 23068672 | tf_op jit(solution)/shard_map/dot_general | solution.py:20
  998.9 4.8 fusion.34
  1003.8 15.9 %reshape.159 = bf16[16,128,8,2,64]{4,3,2,1,0:T(2,128)(2,1)} reshape(bf16[2048,1024]{1,0:T(8,128)(2,1)} %get-tuple-element.20) | data formatting | bytes 8388608 | tf_op jit(solution)/shard_map/reshape.4
  1019.7 15.9 %reshape.160 = bf16[16,128,8,2,64]{4,3,2,1,0:T(2,128)(2,1)} reshape(bf16[2048,1024]{1,0:T(8,128)(2,1)} %get-tuple-element.19) | data formatting | bytes 8388608 | tf_op jit(solution)/shard_map/reshape.5
  1035.5 20.7 %fusion.8 = f32[128,8,2,16,16]{3,4,2,1,0:T(8,128)} fusion(bf16[16,128,8,2,64]{4,3,2,1,0:T(2,128)(2,1)} %reshape.160, bf16[16,128,8,2,64]{4,3,2,1,0:T(2,128)(2,1)} %reshape.159), kind=kOutput, calls=%fused_computation.12 | convolution fusion | flops 67108864 | bytes 10485760 | tf_op jit(solution)/shard_map/ctpjed,cspjed->cpjets/dot_general | solution.py:42
  1056.2 12.4 copy.123
  1068.6 1.3 fusion.35
  1069.9 11.9 copy.125
  1081.8 0.7 copy.126
  1082.5 16.1 %reshape.158 = bf16[16,128,8,2,64]{4,3,2,1,0:T(2,128)(2,1)} reshape(bf16[2048,1024]{1,0:T(8,128)(2,1)} %get-tuple-element.18) | data formatting | bytes 8388608 | tf_op jit(solution)/shard_map/reshape.9
  1098.7 12.1 fusion.7
  1110.7 11.3 copy.127
  1122.1 54.3 %all_to_all.30 = bf16[1,16,128,1024]{2,3,0,1:T(8,128)(2,1)} all-to-all(bf16[1,16,128,1024]{2,3,0,1:T(8,128)(2,1)} %bitcast.72), channel_id=1, replica_groups=mesh['dp'=4,'frame'=2,'space'=4] {'frame'}, dimensions={1} | all-to-all | bytes 8388608 | tf_op jit(solution)/shard_map/all_to_all | solution.py:138
  1176.4 6.4 copy.129
  1182.8 2.8 copy.130
  1185.6 0.0 copy-start.1
  1185.6 1.9 copy-done.1
  1187.5 0.0 copy-done.3
  1187.5 5.7 convert_bitcast_fusion
  1193.2 0.0 reduce-scatter.2.cloned.1.call-update
  1193.3 0.0 all-gather.14.cloned.1.call-start
  1193.3 0.5 all-gather.14.cloned.1.call-update
  1193.8 0.0 all-reduce.2.cloned.1.call-start
  1193.9 29.0 %reduce-scatter.2.cloned.1.call-done = bf16[512,1024]{0,1:T(8,128)(2,1)} async-done(((bf16[1024,1024]{0,1:T(8,128)(2,1)}), bf16[512,1024]{0,1:T(8,128)(2,1)}) %reduce-scatter.2.cloned.1.call-update) | async-done | bytes 1048592 | tf_op jit(solution)/shard_map/reduce_scatter | solution.py:147
  1222.9 0.0 all-reduce.2.cloned.1.call-update
  1222.9 34.6 %all-gather.14.cloned.1.call-done = bf16[1024,1024]{1,0:T(8,128)(2,1)} async-done(((bf16[512,1024]{1,0:T(8,128)(2,1)}), bf16[1024,1024]{1,0:T(8,128)(2,1)}) %all-gather.14.cloned.1.call-update) | async-done | bytes 2097168 | tf_op jit(solution)/shard_map/all_gather | solution.py:143
  1257.5 13.2 convolution_add_fusion
  1270.6 83.8 %all-reduce.2.cloned.1.call-done = bf16[512,1024]{0,1:T(8,128)(2,1)} async-done(((bf16[512,1024]{0,1:T(8,128)(2,1)}), bf16[512,1024]{0,1:T(8,128)(2,1)}) %all-reduce.2.cloned.1.call-update) | async-done | bytes 1048592 | tf_op jit(solution)/shard_map/psum | solution.py:155
  1354.5 2.6 copy.131
  (9 shorter events, 0.0 us)
Async XLA Ops:
  7.2 85.5 %all-gather.6.cloned.1.call-start = ((), (), s32[]{:S(2)}) async-start(), calls=%async_computation.3 | async-start | bytes 9437184 | tf_op jit(solution)/shard_map/all_gather | solution.py:82
  7.9 674.2 %all-gather.8.cloned.1.call-start = ((), (), s32[]{:S(2)}) async-start(), calls=%async_computation.4 | async-start | bytes 41943040 | tf_op jit(solution)/shard_map/all_gather | solution.py:87
  120.5 782.9 %all-gather.10.cloned.1.call-start = ((), (), s32[]{:S(2)}) async-start(), calls=%async_computation.5 | async-start | bytes 3145728 | tf_op jit(solution)/shard_map/all_gather | solution.py:112
  121.3 861.0 %all-gather.12.cloned.1.call-start = ((), (), s32[]{:S(2)}) async-start(), calls=%async_computation.6 | async-start | bytes 9437184 | tf_op jit(solution)/shard_map/all_gather | solution.py:130
  903.5 12.9 copy-start.2
  912.9 3.4 copy-start
  922.0 53.4 %all-to-all-start = ((bf16[1,8,256,1024]{3,1,0,2:T(8,128)(2,1)}), bf16[1,8,256,1024]{3,1,0,2:T(8,128)(2,1)}, u32[]{:S(2)}, u32[]{:S(2)}) async-start(bf16[1,8,256,1024]{3,1,0,2:T(8,128)(2,1)} %copy.115), calls=%async_computation | async-start | bytes 8388608 | tf_op jit(solution)/shard_map/all_to_all | solution.py:120
  927.6 295.3 %reduce-scatter.2.cloned.1.call-start = ((), (), s32[]{:S(2)}) async-start(), calls=%async_computation.8 | async-start | bytes 3145728 | tf_op jit(solution)/shard_map/reduce_scatter | solution.py:147
  1182.8 4.7 copy-start.3
  1185.6 1.9 copy-start.1
  1193.3 64.2 %all-gather.14.cloned.1.call-start = ((), (), s32[]{:S(2)}) async-start(), calls=%async_computation.7 | async-start | bytes 3145728 | tf_op jit(solution)/shard_map/all_gather | solution.py:143
  1193.8 160.6 %all-reduce.2.cloned.1.call-start = ((), (), s32[]{:S(2)}) async-start(), calls=%async_computation.9 | async-start | bytes 2097152 | tf_op jit(solution)/shard_map/psum | solution.py:155
Sparse Core Ops, SparseCore 0:
  9.5 83.0 all-gather.5
  120.6 561.3 all-gather.7
  683.6 31.2 all-gather.9
  716.4 80.3 all-gather.11
  1193.4 29.4 reduce-scatter.1
  1224.3 33.0 all-gather.13
  1261.3 93.0 all-reduce.1
where the time goes:
time: 1370 us; the launch traced here: 1360 us
  waiting for transfers between devices  817 us (60%)
  local copies, waits for them, and re-layouts  218 us (16%)
  matrix products  202 us (15%)
  blocking collectives  54.3 us (4%)
  other arithmetic  51 us (4%)
  between operations  16 us (1%)
    all_gather x1, waiting for transfers between devices, on_device(): shard_block = lax.all_gather(keys_values, 'space', axis=1, tiled=True)  543 us
    psum x1, waiting for transfers between devices, on_device(): grad_out = lax.psum(grad_share, ('dp', 'space')).astype(jnp.float32)  83.8 us
    all_gather x1, waiting for transfers between devices, on_device(): lax.all_gather(spatial_qkv, 'frame', axis=0, tiled=True)  77.4 us
    dot_general x4, matrix products, fold_rows(): return jnp.dot(activations, weight_rows, preferred_element_type=jnp.float32)  58.7 us
    dot_general x1, matrix products, on_device(): jnp.einsum('gqhd,gkhd->ghqk', queries, key_rows, preferred_element_type=j...  55 us
    all_to_all x1, blocking collectives, on_device(): lax.all_to_all(result_rows.reshape(leading + (width,)), 'frame', split_ax...  54.3 us
    dot_general x1, matrix products, on_device(): jnp.einsum('ghqk,gkhd->gqhd', attn_weights.astype(jnp.bfloat16), value_ro...  49.9 us
    another operation x3, local copies, waits for them, and re-layouts  47.9 us
  transfers between devices with their start and end apart: 8, of which 6 were waited for; matrix products, arithmetic and copies ran while one was open for 21% of the time, Pallas kernels for 0%

commit v1 on v0

v1 whole, which is shorter than its diff:
```python
import functools
import math

import jax
import jax.numpy as jnp
from jax import lax
from jax.experimental import pallas as pl
from jax.experimental.pallas import tpu as pltpu
from jax.sharding import PartitionSpec as P

HD = 64
PAIR = 2 * HD

norm_eps = 1e-06
score_scale = 0.125
exp2_scale = score_scale * math.log2(math.e)


def rms_norm(row_block, gain):
    values = row_block.astype(jnp.float32)
    mean_square = jnp.mean(values * values, axis=-1, keepdims=True)
    return (values * lax.rsqrt(mean_square + norm_eps) * gain).astype(jnp.bfloat16)


def fold_rows(activations, weight_rows):
    return jnp.dot(activations, weight_rows, preferred_element_type=jnp.float32)


def frame_visible(lookback, valid_frames, query_pos, key_pos):
    return (
        (key_pos <= query_pos)
        & (query_pos - key_pos < lookback)
        & ((key_pos < valid_frames) | (key_pos == query_pos))
    )


def pair_attention(query, key, value, bias=None):
    low_q = lax.broadcasted_iota(jnp.int32, query.shape, 1) < HD
    low_v = lax.broadcasted_iota(jnp.int32, value.shape, 1) < HD
    none = jnp.zeros_like(query)
    ones = jnp.ones_like(value)
    mixed = []
    for query_one, value_one in (
        (jnp.where(low_q, query, none), jnp.where(low_v, value, ones)),
        (jnp.where(low_q, none, query), jnp.where(low_v, ones, value)),
    ):
        scores = lax.dot_general(
            query_one, key, (((1,), (1,)), ((), ())), preferred_element_type=jnp.float32
        )
        if bias is not None:
            scores = scores + bias
        row_best = jnp.max(scores, axis=-1, keepdims=True)
        weights = jnp.exp2((scores - row_best) * exp2_scale).astype(jnp.bfloat16)
        mixed.append(jnp.dot(weights, value_one, preferred_element_type=jnp.float32))
    first, second = mixed
    top = jnp.where(low_q, first, second)
    bottom = pltpu.roll(jnp.where(low_q, second, first), HD, 1)
    return (top / bottom).astype(jnp.bfloat16)


def spatial_kernel(query_ref, key_ref, value_ref, out_ref, *, step):
    key, value = key_ref[...], value_ref[...]
    for start in range(0, query_ref.shape[0], step):
        out_ref[start : start + step, :] = pair_attention(
            query_ref[start : start + step, :], key, value
        )


def spatial_attention(projected, patches, width):
    rows = projected.shape[0]
    pairs = width // PAIR

    def block(shift):
        return pl.BlockSpec((patches, PAIR), lambda g, j: (g, j + shift * pairs))

    return pl.pallas_call(
        functools.partial(spatial_kernel, step=min(256, patches)),
        grid=(rows // patches, pairs),
        in_specs=[block(0), block(1), block(2)],
        out_specs=block(0),
        out_shape=jax.ShapeDtypeStruct((rows, width), jnp.bfloat16),
        compiler_params=pltpu.CompilerParams(vmem_limit_bytes=48 * 2**20),
        cost_estimate=pl.CostEstimate(
            flops=4 * rows * patches * width,
            bytes_accessed=8 * rows * width,
            transcendentals=rows * patches * width // HD,
        ),
    )(projected, projected, projected)


def temporal_kernel(bias_ref, rows_ref, out_ref, *, width):
    bias = bias_ref[...]
    frames, group, _ = out_ref.shape
    for start in range(0, width, PAIR):
        parts = [
            rows_ref[:, :, shift + start : shift + start + PAIR].reshape(frames * group, PAIR)
            for shift in (0, width, 2 * width)
        ]
        out_ref[:, :, start : start + PAIR] = pair_attention(*parts, bias).reshape(
            frames, group, PAIR
        )


def temporal_attention(projected, lookback, valid_frames, width):
    frames, patches, _ = projected.shape
    group = 16
    spots = frames * group
    row = lax.broadcasted_iota(jnp.int32, (spots, spots), 0)
    column = lax.broadcasted_iota(jnp.int32, (spots, spots), 1)
    seen = frame_visible(lookback, valid_frames, row // group, column // group)
    bias = jnp.where(seen & (row % group == column % group), 0.0, -1e30).astype(jnp.float32)
    return pl.pallas_call(
        functools.partial(temporal_kernel, width=width),
        grid=(patches // group,),
        in_specs=[
            pl.BlockSpec((spots, spots), lambda i: (0, 0)),
            pl.BlockSpec((frames, group, 3 * width), lambda i: (0, i, 0)),
        ],
        out_specs=pl.BlockSpec((frames, group, width), lambda i: (0, i, 0)),
        out_shape=jax.ShapeDtypeStruct((frames, patches, width), jnp.bfloat16),
        compiler_params=pltpu.CompilerParams(vmem_limit_bytes=48 * 2**20),
        cost_estimate=pl.CostEstimate(
            flops=4 * spots * frames * patches * width,
            bytes_accessed=8 * frames * patches * width,
            transcendentals=spots * frames * patches * width // HD,
        ),
    )(bias, projected)


def gather_rows(weight):
    return lax.all_gather(weight, "frame", axis=0, tiled=True)


def spatial_by_frames(tokens, gain, qkv):
    frames_here, patches_here, width = tokens.shape
    whole = lax.all_to_all(tokens, "space", split_axis=0, concat_axis=1, tiled=True)
    frames, patches, _ = whole.shape
    normed = rms_norm(whole.reshape(frames * patches, width), gain)
    projected = fold_rows(normed, qkv).astype(jnp.bfloat16)
    attended = spatial_attention(projected, patches, width).reshape(frames, patches, width)
    return lax.all_to_all(attended, "space", split_axis=1, concat_axis=0, tiled=True)


def spatial_by_heads(tokens, gain, qkv):
    frames_here, patches_here, width = tokens.shape
    parts = lax.axis_size("space")
    normed = rms_norm(tokens.reshape(-1, width), gain)
    projected = fold_rows(normed, qkv).astype(jnp.bfloat16)
    split = projected.reshape(frames_here, patches_here, 3, parts, width // parts)
    whole = lax.all_to_all(split, "space", split_axis=3, concat_axis=1, tiled=True)
    patches = whole.shape[1]
    attended = spatial_attention(
        whole.reshape(frames_here * patches, -1), patches, width // parts
    ).reshape(frames_here, patches, width // parts)
    return lax.all_to_all(attended, "space", split_axis=1, concat_axis=2, tiled=True)


def on_device(
    clip_tokens,
    lookback,
    valid_frames,
    spatial_gain,
    spatial_qkv,
    spatial_out,
    temporal_gain,
    temporal_qkv,
    temporal_out,
    cotangent,
):
    clip_count, frames_here, patches_here, width = clip_tokens.shape
    total_rows = frames_here * patches_here
    by_frames = frames_here % lax.axis_size("space") == 0
    spatial = spatial_by_frames if by_frames else spatial_by_heads
    tokens = clip_tokens[0]
    spatial_attn = spatial(tokens, spatial_gain, gather_rows(spatial_qkv))
    spatial_proj = fold_rows(spatial_attn.reshape(total_rows, width), gather_rows(spatial_out))
    after_spatial = tokens.reshape(total_rows, width).astype(jnp.float32) + spatial_proj
    normed_next = rms_norm(after_spatial, temporal_gain)
    patch_tokens = lax.all_to_all(
        normed_next.reshape(frames_here, patches_here, width),
        "frame",
        split_axis=1,
        concat_axis=0,
        tiled=True,
    )
    frames, patches, _ = patch_tokens.shape
    projected = fold_rows(
        patch_tokens.reshape(frames * patches, width), gather_rows(temporal_qkv)
    ).astype(jnp.bfloat16)
    result_rows = temporal_attention(
        projected.reshape(frames, patches, 3 * width), lookback[0], valid_frames[0], width
    )
    temporal_attn = lax.all_to_all(
        result_rows, "frame", split_axis=0, concat_axis=1, tiled=True
    ).reshape(total_rows, width)
    grad_rows = cotangent.reshape(total_rows, width)
    grad_share = lax.psum_scatter(
        lax.dot_general(
            grad_rows, temporal_attn, (((0,), (0,)), ((), ())), preferred_element_type=jnp.float32
        ).astype(jnp.bfloat16),
        "frame",
        scatter_dimension=0,
        tiled=True,
    )
    grad_out = lax.psum(grad_share, ("dp", "space")).astype(jnp.float32)
    temporal_proj = fold_rows(temporal_attn, gather_rows(temporal_out))
    block_out = (after_spatial + temporal_proj).reshape(clip_tokens.shape)
    return (block_out, grad_out)


def solution(mesh):
    placed = (
        P("dp", "frame", "space", None),
        P("dp"),
        P("dp"),
        P(),
        P("frame", None),
        P("frame", None),
        P(),
        P("frame", None),
        P("frame", None),
        P("dp", "frame", "space", None),
    )
    return jax.shard_map(
        on_device,
        mesh=mesh,
        in_specs=placed,
        out_specs=(P("dp", "frame", "space", None), P("frame", None)),
        check_vma=False,
    )
```

time: 1370 us -> 670 us (0.49)
  waiting for transfers between devices: 817 us -> 378 us
  local copies, waits for them, and re-layouts: 218 us -> 36 us
  matrix products: 202 us -> 66.8 us
  Pallas kernels: 0 us -> 90.6 us
  other arithmetic: 51 us -> 13.1 us
    all_gather x5 -> x4, waiting for transfers between devices: 655 us -> 34.6 us  [gather_rows(): return lax.all_gather(weight, 'frame', axis=0, tiled=True)]
    all_to_all x1 -> x3, waiting for transfers between devices: 46.4 us -> 229 us  [the longest x1 92.7 us: spatial_by_frames(): lax.all_to_all(tokens, 'space', split_axis=0, concat_axis=1, tiled=True)]
    dot_general x4 -> x0, matrix products: 138 us -> none  [the longest x1 55 us: on_device(): jnp.einsum('gqhd,gkhd->ghqk', queries, key_rows, preferred_element_type=j...]
    pallas_call x0 -> x2, Pallas kernels: none -> 90.6 us  [the longest x1 65.8 us: spatial_attention(): pl.pallas_call(functools.partial(spatial_kernel, step=min(256, patches)),...]
    slice x6 -> x0, local copies, waits for them, and re-layouts: 84.6 us -> none  [the longest x2 44.9 us: on_device(): shard_block[:, :, width:].reshape(group_count, count_here, head_count, HD)]
    another operation x3 -> x0, local copies, waits for them, and re-layouts: 47.9 us -> none
    reduce_sum x1 -> x0, other arithmetic: 41.1 us -> none  [on_device(): weight_sum = jnp.sum(attn_weights, axis=-1)]
    convert_element_type x3 -> x1, local copies, waits for them, and re-layouts: 28.2 us -> 4.24 us  [rms_norm(): values = row_block.astype(jnp.float32)]
  transfers between devices with their start and end apart: 8 -> 9, of which waited for: 6 -> 6; matrix products, arithmetic and copies ran while one was open for 21% -> 8% of each run, Pallas kernels for 0% -> 0%
where the time goes in v1:
time: 670 us; the launch traced here: 667 us
  waiting for transfers between devices  378 us (56%)
  Pallas kernels  90.6 us (14%)
  matrix products  66.8 us (10%)
  blocking collectives  48.6 us (7%)
  local copies, waits for them, and re-layouts  36 us (5%)
  starting transfers between devices  17.2 us (3%)
  between operations  15.8 us (2%)
  other arithmetic  13.1 us (2%)
    all_to_all x1, waiting for transfers between devices, spatial_by_frames(): lax.all_to_all(tokens, 'space', split_axis=0, concat_axis=1, tiled=True)  92.7 us
    all_to_all x1, waiting for transfers between devices, spatial_by_frames(): lax.all_to_all(attended, 'space', split_axis=1, concat_axis=0, tiled=True)  91.1 us
    psum x1, waiting for transfers between devices, on_device(): grad_out = lax.psum(grad_share, ('dp', 'space')).astype(jnp.float32)  83.7 us
    pallas_call x1, Pallas kernels, spatial_attention(): pl.pallas_call(functools.partial(spatial_kernel, step=min(256, patches)),...  65.8 us
    dot_general x4, matrix products, fold_rows(): return jnp.dot(activations, weight_rows, preferred_element_type=jnp.float32)  61.1 us
    all_to_all x1, blocking collectives, on_device(): lax.all_to_all(result_rows, 'frame', split_axis=0, concat_axis=1, tiled=T...  48.6 us
    all_to_all x1, waiting for transfers between devices, on_device(): lax.all_to_all(normed_next.reshape(frames_here, patches_here, width), 'fr...  45.2 us
    all_gather x4, waiting for transfers between devices, gather_rows(): return lax.all_gather(weight, 'frame', axis=0, tiled=True)  34.6 us
  transfers between devices with their start and end apart: 9, of which 6 were waited for; matrix products, arithmetic and copies ran while one was open for 8% of the time, Pallas kernels for 0%

profile of v1, /device:TPU:0, one launch (start us, length us, event | category | flops | bytes accessed | tf_op | source)
XLA Modules:
  0.0 666.5 jit_solution(6581903430171151698)
XLA Ops:
  7.2 6.3 all-to-all-start
  13.5 0.0 all-gather.5.cloned.1.call-start
  13.5 0.7 all-gather.5.cloned.1.call-update
  14.2 92.7 %all-to-all-done = bf16[8,256,1024]{2,1,0:T(8,128)(2,1)} async-done(((bf16[8,256,1024]{2,1,0:T(8,128)(2,1)}), bf16[8,256,1024]{2,1,0:T(8,128)(2,1)}, u32[]{:S(2)}, u32[]{:S(2)}) %all-to-all-start) | async-done | bytes 4194336 | tf_op jit(solution)/shard_map/all_to_all | solution.py:136
  106.9 3.2 convert_element_type.61
  110.1 4.2 copy.21
  114.4 0.0 copy-start.2
  114.4 3.1 multiply_reduce_fusion.1
  117.5 0.0 copy-done.2
  117.5 5.4 fusion.1
  123.0 0.0 all-gather.5.cloned.1.call-done
  123.0 19.3 %convolution_convert_fusion.1.query_ref.key_ref.value_ref = bf16[2048,3072]{1,0:T(8,128)(2,1)} fusion(bf16[2048,1024]{1,0:T(8,128)(2,1)} %fusion.1, bf16[1024,3072]{1,0:T(8,128)(2,1)} %all-gather.5.cloned.1.call-done), kind=kOutput, calls=%fused_computation.1 | convolution fusion | flops 12891193344 | bytes 23068672 | tf_op jit(solution)/shard_map/dot_general | solution.py:26
  142.3 65.8 %shard_map.113 = bf16[2048,1024]{1,0:T(8,128)(2,1)S(1)} custom-call(bf16[2048,3072]{1,0:T(8,128)(2,1)} %convolution_convert_fusion.1.query_ref.key_ref.value_ref, bf16[2048,3072]{1,0:T(8,128)(2,1)} %convolution_convert_fusion.1.query_ref.key_ref.value_ref, bf16[2048,3072]{1,0:T(8,128)(2,1)} %convolution_convert_fusion.1.query_ref.key_ref.value_ref), custom_call_target="tpu_custom_call" | custom-call | flops 8589934592 | bytes 16777216 | tf_op jit(solution)/shard_map/pallas_call | solution.py:76
  208.1 6.3 copy.23
  214.4 4.9 all-to-all-start.1
  219.3 0.0 all-gather.7.cloned.1.call-start
  219.3 0.7 all-gather.7.cloned.1.call-update
  220.0 0.0 all-gather.9.cloned.1.call-start
  220.1 0.7 all-gather.9.cloned.1.call-update
  220.8 91.1 %all-to-all-done.1 = bf16[2,1024,1024]{2,0,1:T(2,128)(2,1)} async-done(((bf16[2,1024,1024]{2,0,1:T(2,128)(2,1)}), bf16[2,1024,1024]{2,0,1:T(2,128)(2,1)}, u32[]{:S(2)}, u32[]{:S(2)}) %all-to-all-start.1) | async-done | bytes 4194336 | tf_op jit(solution)/shard_map/all_to_all | solution.py:141
  311.9 3.5 copy.24
  315.4 2.5 copy.25
  317.9 0.0 all-gather.7.cloned.1.call-done
  317.9 0.0 copy-start.3
  317.9 9.2 %multiply_reduce_fusion = (f32[2048]{0:T(1024)S(1)}, f32[2048,1024]{1,0:T(8,128)S(1)}) fusion(bf16[2048,1024]{1,0:T(8,128)(2,1)} %bitcast.60, bf16[1024,1024]{1,0:T(8,128)(2,1)} %all-gather.7.cloned.1.call-done, bf16[1,8,256,1024]{3,2,1,0:T(8,128)(2,1)} %param.10), kind=kOutput, calls=%fused_computation.7 | convolution fusion | flops 4303353856 | bytes 18882560 | tf_op jit(solution)/shard_map/dot_general | solution.py:26
  327.1 0.0 copy-start
  327.1 0.0 copy-done.3
  327.1 1.1 multiply_convert_fusion
  328.2 2.3 copy-done
  330.5 4.3 copy.26
  334.8 5.6 all-to-all-start.2
  340.4 0.0 reduce-scatter.2.cloned.1.call-start
  341.8 0.3 fusion.7.bias_ref
  342.1 45.2 %all-to-all-done.2 = bf16[8,256,1024]{2,0,1:T(8,128)(2,1)} async-done(((bf16[8,256,1024]{2,0,1:T(8,128)(2,1)}), bf16[8,256,1024]{2,0,1:T(8,128)(2,1)}, u32[]{:S(2)}, u32[]{:S(2)}) %all-to-all-start.2) | async-done | bytes 4194336 | tf_op jit(solution)/shard_map/all_to_all | solution.py:179
  387.3 6.5 copy.28
  393.8 0.0 all-gather.9.cloned.1.call-done
  393.8 19.3 %convolution_convert_fusion = bf16[2048,3072]{1,0:T(8,128)(2,1)} fusion(bf16[2048,1024]{1,0:T(8,128)(2,1)} %bitcast.61, bf16[1024,3072]{1,0:T(8,128)(2,1)} %all-gather.9.cloned.1.call-done), kind=kOutput, calls=%fused_computation | convolution fusion | flops 12891193344 | bytes 23068672 | tf_op jit(solution)/shard_map/dot_general | solution.py:26
  413.2 24.8 %shard_map.114 = bf16[16,128,1024]{2,1,0:T(8,128)(2,1)S(1)} custom-call(f32[256,256]{1,0:T(8,128)S(1)} %fusion.7.bias_ref, bf16[16,128,3072]{2,1,0:T(8,128)(2,1)} %bitcast.56), custom_call_target="tpu_custom_call" | custom-call | flops 2147483648 | bytes 16777216 | tf_op jit(solution)/shard_map/pallas_call | solution.py:112
  438.0 48.6 %all_to_all.54 = bf16[16,128,1024]{2,1,0:T(8,128)(2,1)S(1)} all-to-all(bf16[16,128,1024]{2,1,0:T(8,128)(2,1)S(1)} %shard_map.114), channel_id=1, replica_groups=mesh['dp'=4,'frame'=2,'space'=4] {'frame'}, dimensions={0} | all-to-all | bytes 8388608 | tf_op jit(solution)/shard_map/all_to_all | solution.py:193
  486.6 0.0 copy-start.4
  486.6 0.6 copy.29
  487.2 0.0 copy-start.1
  487.2 2.1 copy-done.1
  489.4 1.0 copy-done.4
  490.3 5.7 convert_bitcast_fusion
  496.1 0.0 reduce-scatter.2.cloned.1.call-update
  496.1 0.0 all-gather.11.cloned.1.call-start
  496.1 0.5 all-gather.11.cloned.1.call-update
  496.7 0.3 all-reduce.2.cloned.1.call-start
  496.9 28.5 %reduce-scatter.2.cloned.1.call-done = bf16[512,1024]{0,1:T(8,128)(2,1)} async-done(((bf16[1024,1024]{0,1:T(8,128)(2,1)}), bf16[512,1024]{0,1:T(8,128)(2,1)}) %reduce-scatter.2.cloned.1.call-update) | async-done | bytes 1048592 | tf_op jit(solution)/shard_map/reduce_scatter | solution.py:197
  525.4 0.0 all-reduce.2.cloned.1.call-update
  525.4 34.6 %all-gather.11.cloned.1.call-done = bf16[1024,1024]{1,0:T(8,128)(2,1)} async-done(((bf16[512,1024]{1,0:T(8,128)(2,1)}), bf16[1024,1024]{1,0:T(8,128)(2,1)}) %all-gather.11.cloned.1.call-update) | async-done | bytes 2097168 | tf_op jit(solution)/shard_map/all_gather | solution.py:131
  560.0 13.2 %convolution_add_fusion = f32[2048,1024]{1,0:T(8,128)} fusion(f32[2048,1024]{1,0:T(8,128)} %copy-done, bf16[2048,1024]{1,0:T(8,128)(2,1)} %bitcast.59, bf16[1024,1024]{1,0:T(8,128)(2,1)} %all-gather.11.cloned.1.call-done), kind=kOutput, calls=%fused_computation.9 | convolution fusion | flops 4297064448 | bytes 23068672 | tf_op jit(solution)/shard_map/dot_general | solution.py:26
  573.2 83.7 %all-reduce.2.cloned.1.call-done = bf16[512,1024]{0,1:T(8,128)(2,1)} async-done(((bf16[512,1024]{0,1:T(8,128)(2,1)}), bf16[512,1024]{0,1:T(8,128)(2,1)}) %all-reduce.2.cloned.1.call-update) | async-done | bytes 1048592 | tf_op jit(solution)/shard_map/psum | solution.py:205
  656.9 2.6 copy.30
  (8 shorter events, 0.1 us)
Async XLA Ops:
  7.2 99.8 %all-to-all-start = ((bf16[8,256,1024]{2,1,0:T(8,128)(2,1)}), bf16[8,256,1024]{2,1,0:T(8,128)(2,1)}, u32[]{:S(2)}, u32[]{:S(2)}) async-start(bf16[8,256,1024]{2,1,0:T(8,128)(2,1)} %bitcast.57), calls=%async_computation | async-start | bytes 8388608 | tf_op jit(solution)/shard_map/all_to_all | solution.py:136
  13.5 109.5 %all-gather.5.cloned.1.call-start = ((), (), s32[]{:S(2)}) async-start(), calls=%async_computation.5 | async-start | bytes 9437184 | tf_op jit(solution)/shard_map/all_gather | solution.py:131
  114.4 3.1 copy-start.2
  214.4 97.5 %all-to-all-start.1 = ((bf16[2,1024,1024]{2,0,1:T(2,128)(2,1)}), bf16[2,1024,1024]{2,0,1:T(2,128)(2,1)}, u32[]{:S(2)}, u32[]{:S(2)}) async-start(bf16[2,1024,1024]{2,0,1:T(2,128)(2,1)} %copy.23), calls=%async_computation.1 | async-start | bytes 8388608 | tf_op jit(solution)/shard_map/all_to_all | solution.py:141
  219.3 98.6 %all-gather.7.cloned.1.call-start = ((), (), s32[]{:S(2)}) async-start(), calls=%async_computation.6 | async-start | bytes 3145728 | tf_op jit(solution)/shard_map/all_gather | solution.py:131
  220.0 173.8 %all-gather.9.cloned.1.call-start = ((), (), s32[]{:S(2)}) async-start(), calls=%async_computation.7 | async-start | bytes 9437184 | tf_op jit(solution)/shard_map/all_gather | solution.py:131
  317.9 9.3 %copy-start.3 = (f32[1024]{0:T(1024)S(1)}, f32[1024]{0:T(1024)}, u32[]{:S(2)}) copy-start(f32[1024]{0:T(1024)} %param.16) | copy-start | bytes 12292
  327.1 3.4 copy-start
  334.8 52.5 %all-to-all-start.2 = ((bf16[8,256,1024]{2,0,1:T(8,128)(2,1)}), bf16[8,256,1024]{2,0,1:T(8,128)(2,1)}, u32[]{:S(2)}, u32[]{:S(2)}) async-start(bf16[8,256,1024]{2,0,1:T(8,128)(2,1)} %copy.26), calls=%async_computation.2 | async-start | bytes 8388608 | tf_op jit(solution)/shard_map/all_to_all | solution.py:179
  340.4 185.0 %reduce-scatter.2.cloned.1.call-start = ((), (), s32[]{:S(2)}) async-start(), calls=%async_computation.9 | async-start | bytes 3145728 | tf_op jit(solution)/shard_map/reduce_scatter | solution.py:197
  486.6 3.7 copy-start.4
  487.2 2.1 copy-start.1
  496.1 64.0 %all-gather.11.cloned.1.call-start = ((), (), s32[]{:S(2)}) async-start(), calls=%async_computation.8 | async-start | bytes 3145728 | tf_op jit(solution)/shard_map/all_gather | solution.py:131
  496.7 160.2 %all-reduce.2.cloned.1.call-start = ((), (), s32[]{:S(2)}) async-start(), calls=%async_computation.10 | async-start | bytes 2097152 | tf_op jit(solution)/shard_map/psum | solution.py:205
Sparse Core Ops, SparseCore 0:
  15.9 81.8 all-gather.4
  221.7 34.5 all-gather.6
  257.8 80.3 all-gather.8
  496.2 29.1 reduce-scatter.1
  526.9 33.1 all-gather.10
  563.8 93.0 all-reduce.1

commit v2 on v1

--- a/solution.py
+++ b/solution.py
@@ -131,6 +131,19 @@
     return lax.all_gather(weight, "frame", axis=0, tiled=True)
 
 
+def swap_frames(rows, to_patches):
+    split, concat = (1, 0) if to_patches else (0, 1)
+    if lax.axis_size("frame") != 2:
+        return lax.all_to_all(rows, "frame", split_axis=split, concat_axis=concat, tiled=True)
+    first = lax.axis_index("frame") == 0
+    low, high = jnp.split(rows, 2, axis=split)
+    kept = jnp.where(first, low, high)
+    came = lax.ppermute(jnp.where(first, high, low), "frame", [(0, 1), (1, 0)])
+    return jnp.concatenate(
+        [jnp.where(first, kept, came), jnp.where(first, came, kept)], axis=concat
+    )
+
+
 def spatial_by_frames(tokens, gain, qkv):
     frames_here, patches_here, width = tokens.shape
     whole = lax.all_to_all(tokens, "space", split_axis=0, concat_axis=1, tiled=True)
@@ -168,44 +181,58 @@
     cotangent,
 ):
     clip_count, frames_here, patches_here, width = clip_tokens.shape
-    total_rows = frames_here * patches_here
-    by_frames = frames_here % lax.axis_size("space") == 0
+    parts, frame_parts = lax.axis_size("space"), lax.axis_size("frame")
+    by_frames = frames_here % parts == 0
     spatial = spatial_by_frames if by_frames else spatial_by_heads
-    tokens = clip_tokens[0]
-    spatial_attn = spatial(tokens, spatial_gain, gather_rows(spatial_qkv))
-    spatial_proj = fold_rows(spatial_attn.reshape(total_rows, width), gather_rows(spatial_out))
-    after_spatial = tokens.reshape(total_rows, width).astype(jnp.float32) + spatial_proj
-    normed_next = rms_norm(after_spatial, temporal_gain)
-    patch_tokens = lax.all_to_all(
-        normed_next.reshape(frames_here, patches_here, width),
-        "frame",
-        split_axis=1,
-        concat_axis=0,
-        tiled=True,
-    )
-    frames, patches, _ = patch_tokens.shape
+    chunks = 2 if by_frames and frames_here % (2 * parts) == 0 else 1
+    step = frames_here // chunks
+    spatial_weights = gather_rows(spatial_qkv)
+    spatial_out_rows = gather_rows(spatial_out)
+    temporal_weights = gather_rows(temporal_qkv)
+    temporal_out_rows = gather_rows(temporal_out)
+    after_parts, patch_parts = [], []
+    for start in range(0, frames_here, step):
+        tokens = clip_tokens[0, start : start + step]
+        spatial_attn = spatial(tokens, spatial_gain, spatial_weights)
+        spatial_proj = fold_rows(spatial_attn.reshape(-1, width), spatial_out_rows)
+        after_rows = tokens.reshape(-1, width).astype(jnp.float32) + spatial_proj
+        after_parts.append(after_rows)
+        patch_tokens = swap_frames(
+            rms_norm(after_rows, temporal_gain).reshape(step, patches_here, width), True
+        )
+        patch_parts.append(patch_tokens.reshape(frame_parts, step, -1, width))
+    grad_rows = swap_frames(cotangent[0], True).reshape(-1, width)
+    patch_tokens = jnp.concatenate(patch_parts, axis=1)
+    frames = frame_parts * frames_here
+    patches = patch_tokens.shape[2]
     projected = fold_rows(
-        patch_tokens.reshape(frames * patches, width), gather_rows(temporal_qkv)
+        patch_tokens.reshape(frames * patches, width), temporal_weights
     ).astype(jnp.bfloat16)
+    projected, temporal_out_rows, grad_rows = lax.optimization_barrier(
+        (projected, temporal_out_rows, grad_rows)
+    )
     result_rows = temporal_attention(
         projected.reshape(frames, patches, 3 * width), lookback[0], valid_frames[0], width
     )
-    temporal_attn = lax.all_to_all(
-        result_rows, "frame", split_axis=0, concat_axis=1, tiled=True
-    ).reshape(total_rows, width)
-    grad_rows = cotangent.reshape(total_rows, width)
     grad_share = lax.psum_scatter(
         lax.dot_general(
-            grad_rows, temporal_attn, (((0,), (0,)), ((), ())), preferred_element_type=jnp.float32
+            grad_rows,
+            result_rows.reshape(frames * patches, width),
+            (((0,), (0,)), ((), ())),
+            preferred_element_type=jnp.float32,
         ).astype(jnp.bfloat16),
         "frame",
         scatter_dimension=0,
         tiled=True,
     )
     grad_out = lax.psum(grad_share, ("dp", "space")).astype(jnp.float32)
-    temporal_proj = fold_rows(temporal_attn, gather_rows(temporal_out))
-    block_out = (after_spatial + temporal_proj).reshape(clip_tokens.shape)
-    return (block_out, grad_out)
+    temporal_attn = swap_frames(result_rows, False)
+    block_parts = []
+    for index, after_rows in enumerate(after_parts):
+        rows = temporal_attn[index * step : (index + 1) * step].reshape(-1, width)
+        summed = after_rows + fold_rows(rows, temporal_out_rows)
+        block_parts.append(summed.reshape(1, step, patches_here, width))
+    return (jnp.concatenate(block_parts, axis=1), grad_out)
 
 
 def solution(mesh):

time: 670 us -> 634 us (0.946); the launches traced: 667 us -> 624 us
  waiting for transfers between devices: 378 us -> 283 us
  other arithmetic: 13.1 us -> 56.7 us
    ppermute x0 -> x4, waiting for transfers between devices: none -> 114 us  [swap_frames(): came = lax.ppermute(jnp.where(first, high, low), 'frame', [(0, 1), (1, 0)])]
    all_to_all x1 -> x2, waiting for transfers between devices: 91.1 us -> 37.3 us  [spatial_by_frames(): lax.all_to_all(attended, 'space', split_axis=1, concat_axis=0, tiled=True)]
    all_to_all x1, waiting for transfers between devices: 92.7 us -> 45.4 us  [spatial_by_frames(): lax.all_to_all(tokens, 'space', split_axis=0, concat_axis=1, tiled=True)]
    all_to_all x1 -> x0, waiting for transfers between devices: 45.2 us -> none  [on_device(): lax.all_to_all(normed_next.reshape(frames_here, patches_here, width), 'fr...]
    all_gather x4, waiting for transfers between devices: 34.6 us -> 0.01 us  [gather_rows(): return lax.all_gather(weight, 'frame', axis=0, tiled=True)]
    reduce_scatter x1, waiting for transfers between devices: 28.5 us -> 0.01 us  [on_device(): lax.psum_scatter(lax.dot_general(grad_rows, result_rows.reshape(frames *...]
    unnamed x0 -> x4, other arithmetic: none -> 26.9 us
    unnamed x12 -> x37, local copies, waits for them, and re-layouts: 7.97 us -> 21.7 us
  transfers between devices with their start and end apart: 9 -> 13, of which waited for: 6 -> 7; matrix products, arithmetic and copies ran while one was open for 8% -> 23% of each run, Pallas kernels for 0% -> 11%
where the time goes in v2:
time: 634 us; the launch traced here: 624 us
  waiting for transfers between devices  283 us (45%)
  Pallas kernels  91.7 us (14%)
  matrix products  65.2 us (10%)
  other arithmetic  56.7 us (9%)
  blocking collectives  54.3 us (9%)
  local copies, waits for them, and re-layouts  37.7 us (6%)
  starting transfers between devices  18.6 us (3%)
  between operations  16.2 us (3%)
    ppermute x4, waiting for transfers between devices, swap_frames(): came = lax.ppermute(jnp.where(first, high, low), 'frame', [(0, 1), (1, 0)])  114 us
    psum x1, waiting for transfers between devices, on_device(): grad_out = lax.psum(grad_share, ('dp', 'space')).astype(jnp.float32)  84.6 us
    pallas_call x2, Pallas kernels, spatial_attention(): pl.pallas_call(functools.partial(spatial_kernel, step=min(256, patches)),...  66.7 us
    dot_general x7, matrix products, fold_rows(): return jnp.dot(activations, weight_rows, preferred_element_type=jnp.float32)  59.5 us
    all_to_all x1, blocking collectives, spatial_by_frames(): lax.all_to_all(tokens, 'space', split_axis=0, concat_axis=1, tiled=True)  54.3 us
    all_to_all x1, waiting for transfers between devices, spatial_by_frames(): lax.all_to_all(tokens, 'space', split_axis=0, concat_axis=1, tiled=True)  45.4 us
    all_to_all x2, waiting for transfers between devices, spatial_by_frames(): lax.all_to_all(attended, 'space', split_axis=1, concat_axis=0, tiled=True)  37.3 us
    unnamed x4, other arithmetic  26.9 us
  transfers between devices with their start and end apart: 13, of which 7 were waited for; matrix products, arithmetic and copies ran while one was open for 23% of the time, Pallas kernels for 11%

profile of v2, /device:TPU:0, one launch (start us, length us, event | category | flops | bytes accessed | tf_op | source)
XLA Modules:
  0.0 623.6 jit_solution(16007088019336215911)
XLA Ops:
  7.2 0.7 all-gather.5.cloned.1.call-update
  7.9 5.5 slice_bitcast_fusion.1
  13.4 54.3 %all_to_all.16 = bf16[4,256,1024]{2,1,0:T(8,128)(2,1)S(1)} all-to-all(bf16[4,256,1024]{2,1,0:T(8,128)(2,1)S(1)} %get-tuple-element.14), channel_id=1, replica_groups=mesh['dp'=4,'frame'=2,'space'=4] {'space'}, dimensions={0} | all-to-all | bytes 4194304 | tf_op jit(solution)/shard_map/all_to_all | solution.py:149
  67.7 4.5 all-to-all-start.2
  72.3 0.7 all-gather.7.cloned.1.call-update
  73.0 0.7 all-gather.9.cloned.1.call-update
  73.7 0.5 multiply_reduce_fusion.3
  74.2 45.4 %all-to-all-done.2 = bf16[4,256,1024]{2,1,0:T(8,128)(2,1)} async-done(((bf16[4,256,1024]{2,1,0:T(8,128)(2,1)}), bf16[4,256,1024]{2,1,0:T(8,128)(2,1)}, u32[]{:S(2)}, u32[]{:S(2)}) %all-to-all-start.2) | async-done | bytes 2097184 | tf_op jit(solution)/shard_map/all_to_all | solution.py:149
  119.6 2.1 multiply_reduce_fusion.1
  121.7 3.8 fusion.3
  125.5 11.1 %convolution_convert_fusion.2.query_ref.key_ref.value_ref = bf16[1024,3072]{1,0:T(8,128)(2,1)} fusion(bf16[1024,1024]{1,0:T(8,128)(2,1)} %get-tuple-element.24, bf16[1024,3072]{1,0:T(8,128)(2,1)} %all-gather.5.cloned.1.call-done), kind=kOutput, calls=%fused_computation.3 | convolution fusion | flops 6445596672 | bytes 14680064 | tf_op jit(solution)/shard_map/dot_general | solution.py:26
  136.6 33.4 %shard_map.113 = bf16[1024,1024]{1,0:T(8,128)(2,1)S(1)} custom-call(bf16[1024,3072]{1,0:T(8,128)(2,1)} %convolution_convert_fusion.2.query_ref.key_ref.value_ref, bf16[1024,3072]{1,0:T(8,128)(2,1)} %convolution_convert_fusion.2.query_ref.key_ref.value_ref, bf16[1024,3072]{1,0:T(8,128)(2,1)} %convolution_convert_fusion.2.query_ref.key_ref.value_ref), custom_call_target="tpu_custom_call" | custom-call | flops 4294967296 | bytes 8388608 | tf_op jit(solution)/shard_map/pallas_call | solution.py:76
  170.0 5.2 copy.39
  175.2 0.5 broadcast.142
  175.8 12.8 %reduce.9 = bf16[1024,1024]{1,0:T(8,128)(2,1)S(1)} reduce(bf16[1024,1,1024]{2,1,0:T(2,128)(2,1)} %bitcast.90, bf16[]{:T(256)} %broadcast.142), dimensions={1}, to_apply=%bitcast.80.reduce_sub_computation | reduce | bytes 4194306
  188.6 3.3 reshape.162
  191.8 3.6 all-to-all-start.1
  195.4 11.1 %convolution_convert_fusion.1.query_ref.key_ref.value_ref = bf16[1024,3072]{1,0:T(8,128)(2,1)} fusion(bf16[1024,1024]{1,0:T(8,128)(2,1)} %get-tuple-element.25, bf16[1024,3072]{1,0:T(8,128)(2,1)} %all-gather.5.cloned.1.call-done), kind=kOutput, calls=%fused_computation.2 | convolution fusion | flops 6445596672 | bytes 14680064 | tf_op jit(solution)/shard_map/dot_general | solution.py:26
  206.5 33.3 %shard_map.114 = bf16[1024,1024]{1,0:T(8,128)(2,1)S(1)} custom-call(bf16[1024,3072]{1,0:T(8,128)(2,1)} %convolution_convert_fusion.1.query_ref.key_ref.value_ref, bf16[1024,3072]{1,0:T(8,128)(2,1)} %convolution_convert_fusion.1.query_ref.key_ref.value_ref, bf16[1024,3072]{1,0:T(8,128)(2,1)} %convolution_convert_fusion.1.query_ref.key_ref.value_ref), custom_call_target="tpu_custom_call" | custom-call | flops 4294967296 | bytes 8388608 | tf_op jit(solution)/shard_map/pallas_call | solution.py:76
  239.8 5.2 copy.38
  245.0 14.1 %reduce.8 = bf16[1024,1024]{1,0:T(8,128)(2,1)} reduce(bf16[1024,1,1024]{2,1,0:T(2,128)(2,1)} %bitcast.91, bf16[]{:T(256)} %broadcast.142), dimensions={1}, to_apply=%bitcast.79.reduce_sub_computation | reduce | bytes 4194306
  259.1 4.5 reshape.160
  263.6 5.0 all-to-all-start.3
  268.6 3.8 broadcast_select_fusion.6
  272.4 1.5 collective-permute-start.2
  275.3 3.3 reshape.163
  278.6 37.3 %all-to-all-done.3 = bf16[4,2,131072]{2,1,0:T(2,128)(2,1)} async-done(((bf16[4,2,131072]{2,1,0:T(2,128)(2,1)}), bf16[4,2,131072]{2,1,0:T(2,128)(2,1)}, u32[]{:S(2)}, u32[]{:S(2)}) %all-to-all-start.3) | async-done | bytes 2097184 | tf_op jit(solution)/shard_map/all_to_all | solution.py:154
  315.9 4.9 reshape.161
  320.9 5.5 multiply_reduce_fusion.2
  326.5 2.6 multiply_reduce_fusion
  329.2 1.0 multiply_convert_fusion.1
  330.2 1.0 copy-done.3
  331.1 0.1 broadcast_select_fusion.14
  331.3 1.6 collective-permute-start
  332.9 0.3 fusion.20.bias_ref
  333.1 0.1 broadcast_select_fusion.10
  333.2 0.6 collective-permute-start.1
  333.8 9.9 %collective-permute-done.2 = bf16[8,128,1024]{2,1,0:T(8,128)(2,1)} collective-permute-done((bf16[8,128,1024]{2,1,0:T(8,128)(2,1)}, bf16[8,128,1024]{2,1,0:T(8,128)(2,1)}, u32[]{:S(2)}, u32[]{:S(2)}) %collective-permute-start.2) | collective-permute-done | bytes 2097184 | tf_op jit(solution)/shard_map/ppermute | solution.py:141
  343.7 2.0 broadcast_select_fusion.5
  345.7 2.4 pad_maximum_fusion.2
  348.1 18.0 %collective-permute-done = bf16[4,128,1024]{2,1,0:T(8,128)(2,1)S(1)} collective-permute-done((bf16[4,128,1024]{2,1,0:T(8,128)(2,1)S(1)}, bf16[4,128,1024]{2,1,0:T(8,128)(2,1)S(1)}, u32[]{:S(2)}, u32[]{:S(2)}) %collective-permute-start) | collective-permute-done | bytes 1048608 | tf_op jit(solution)/shard_map/ppermute | solution.py:141
  366.1 0.2 broadcast_select_fusion.13
  366.3 0.2 pad_maximum_fusion.4
  366.5 19.8 %collective-permute-done.1 = bf16[4,128,1024]{2,1,0:T(8,128)(2,1)S(1)} collective-permute-done((bf16[4,128,1024]{2,1,0:T(8,128)(2,1)S(1)}, bf16[4,128,1024]{2,1,0:T(8,128)(2,1)S(1)}, u32[]{:S(2)}, u32[]{:S(2)}) %collective-permute-start.1) | collective-permute-done | bytes 1048608 | tf_op jit(solution)/shard_map/ppermute | solution.py:141
  386.2 0.2 broadcast_select_fusion.9
  386.4 0.2 pad_maximum_fusion.5
  386.6 2.4 pad_maximum_fusion.1
  389.0 19.6 %convolution_convert_fusion = bf16[2048,3072]{1,0:T(8,128)(2,1)} fusion(bf16[2048,1024]{1,0:T(8,128)(2,1)} %bitcast.100, bf16[1024,3072]{1,0:T(8,128)(2,1)} %all-gather.9.cloned.1.call-done), kind=kOutput, calls=%fused_computation | convolution fusion | flops 12891193344 | bytes 23068672 | tf_op jit(solution)/shard_map/dot_general | solution.py:26
  408.6 25.0 %shard_map.115 = bf16[16,128,1024]{2,1,0:T(8,128)(2,1)S(1)} custom-call(f32[256,256]{1,0:T(8,128)S(1)} %fusion.20.bias_ref, bf16[16,128,3072]{2,1,0:T(8,128)(2,1)} %bitcast.94), custom_call_target="tpu_custom_call" | custom-call | flops 2147483648 | bytes 16777216 | tf_op jit(solution)/shard_map/pallas_call | solution.py:112
  433.6 1.9 copy-done
  435.5 5.7 convolution_convert_fusion.3
  441.3 0.0 all-reduce.2.cloned.1.call-start
  441.4 2.6 broadcast_select_fusion.2
  443.9 1.6 collective-permute-start.3
  445.5 66.2 %collective-permute-done.3 = bf16[8,128,1024]{2,1,0:T(8,128)(2,1)S(1)} collective-permute-done((bf16[8,128,1024]{2,1,0:T(8,128)(2,1)S(1)}, bf16[8,128,1024]{2,1,0:T(8,128)(2,1)S(1)}, u32[]{:S(2)}, u32[]{:S(2)}) %collective-permute-start.3) | collective-permute-done | bytes 2097184 | tf_op jit(solution)/shard_map/ppermute | solution.py:141
  511.8 0.4 broadcast_select_fusion.1
  512.2 0.6 fusion.4
  512.8 1.5 copy-done.5
  514.3 0.7 copy-done.13
  515.0 4.3 convolution_add_fusion.1
  519.4 5.3 convolution_add_fusion
  524.7 4.2 pad_maximum_fusion
  528.9 84.6 %all-reduce.2.cloned.1.call-done = bf16[512,1024]{1,0:T(8,128)(2,1)} async-done(((bf16[512,1024]{1,0:T(8,128)(2,1)}), bf16[512,1024]{1,0:T(8,128)(2,1)}) %all-reduce.2.cloned.1.call-update) | async-done | bytes 1048592 | tf_op jit(solution)/shard_map/psum | solution.py:228
  613.5 2.8 convert_element_type.77
  (48 shorter events, 0.3 us)
Async XLA Ops:
  7.2 118.4 %all-gather.5.cloned.1.call-start = ((), (), s32[]{:S(2)}) async-start(), calls=%async_computation.5 | async-start | bytes 9437184 | tf_op jit(solution)/shard_map/all_gather | solution.py:131
  67.7 51.9 %all-to-all-start.2 = ((bf16[4,256,1024]{2,1,0:T(8,128)(2,1)}), bf16[4,256,1024]{2,1,0:T(8,128)(2,1)}, u32[]{:S(2)}, u32[]{:S(2)}) async-start(bf16[4,256,1024]{2,1,0:T(8,128)(2,1)} %get-tuple-element.15), calls=%async_computation.2 | async-start | bytes 4194304 | tf_op jit(solution)/shard_map/all_to_all | solution.py:149
  72.2 248.7 %all-gather.7.cloned.1.call-start = ((), (), s32[]{:S(2)}) async-start(), calls=%async_computation.6 | async-start | bytes 3145728 | tf_op jit(solution)/shard_map/all_gather | solution.py:131
  73.0 316.0 %all-gather.9.cloned.1.call-start = ((), (), s32[]{:S(2)}) async-start(), calls=%async_computation.7 | async-start | bytes 9437184 | tf_op jit(solution)/shard_map/all_gather | solution.py:131
  73.7 48.0 %copy-start.12 = (f32[1024]{0:T(1024)S(1)}, f32[1024]{0:T(1024)}, u32[]{:S(2)}) copy-start(f32[1024]{0:T(1024)} %param.13) | copy-start | bytes 12292
  191.8 71.8 %all-to-all-start.1 = ((bf16[4,2,131072]{2,1,0:T(2,128)(2,1)}), bf16[4,2,131072]{2,1,0:T(2,128)(2,1)S(1)}, u32[]{:S(2)}, u32[]{:S(2)}) async-start(bf16[4,2,131072]{2,1,0:T(2,128)(2,1)} %reshape.162), calls=%async_computation.1 | async-start | bytes 4194304 | tf_op jit(solution)/shard_map/all_to_all | solution.py:154
  263.6 52.4 %all-to-all-start.3 = ((bf16[4,2,131072]{2,1,0:T(2,128)(2,1)}), bf16[4,2,131072]{2,1,0:T(2,128)(2,1)}, u32[]{:S(2)}, u32[]{:S(2)}) async-start(bf16[4,2,131072]{2,1,0:T(2,128)(2,1)} %reshape.160), calls=%async_computation.3 | async-start | bytes 4194304 | tf_op jit(solution)/shard_map/all_to_all | solution.py:154
  268.6 140.0 %all-gather.11.cloned.1.call-start = ((), (), s32[]{:S(2)}) async-start(), calls=%async_computation.8 | async-start | bytes 3145728 | tf_op jit(solution)/shard_map/all_gather | solution.py:131
  272.4 71.4 %collective-permute-start.2 = (bf16[8,128,1024]{2,1,0:T(8,128)(2,1)}, bf16[8,128,1024]{2,1,0:T(8,128)(2,1)}, u32[]{:S(2)}, u32[]{:S(2)}) collective-permute-start(bf16[8,128,1024]{2,1,0:T(8,128)(2,1)} %broadcast_select_fusion.6), channel_id=1, source_target_pairs={{0,4},{4,0},{1,5},{5,1},{2,6},{6,2},{3,7},{7,3},{8,12},{12,8},{9,1... | collective-permute-start | bytes 6291464 | tf_op jit(solution)/shard_map/ppermute | solution.py:141
  273.9 245.4 %reduce-scatter.2.cloned.1.call-start = ((), (), s32[]{:S(2)}) async-start(), calls=%async_computation.9 | async-start | bytes 3145728 | tf_op jit(solution)/shard_map/reduce_scatter | solution.py:217
  278.6 42.3 %copy-start.10 = (bf16[1,4,256,1024]{3,2,1,0:T(8,128)(2,1)S(1)}, bf16[1,4,256,1024]{3,2,1,0:T(8,128)(2,1)}, u32[]{:S(2)}) copy-start(bf16[1,4,256,1024]{3,2,1,0:T(8,128)(2,1)} %get-tuple-element.17) | copy-start | bytes 6291460
  320.9 5.6 copy-start.6
  320.9 5.6 copy-start.9
  320.9 5.6 copy-start.14
  326.4 2.7 copy-start.4
  326.5 2.7 copy-start.11
  329.1 2.0 copy-start.3
  331.1 12.6 %copy-start.2 = (bf16[1,8,256,1024]{3,2,1,0:T(8,128)(2,1)S(1)}, bf16[1,8,256,1024]{3,2,1,0:T(8,128)(2,1)}, u32[]{:S(2)}) copy-start(bf16[1,8,256,1024]{3,2,1,0:T(8,128)(2,1)} %param.19) | copy-start | bytes 12582916
  331.3 34.8 %collective-permute-start = (bf16[4,128,1024]{2,1,0:T(8,128)(2,1)S(1)}, bf16[4,128,1024]{2,1,0:T(8,128)(2,1)S(1)}, u32[]{:S(2)}, u32[]{:S(2)}) collective-permute-start(bf16[4,128,1024]{2,1,0:T(8,128)(2,1)S(1)} %broadcast_select_fusion.14), channel_id=1, source_target_pairs={{0,4},{4,0},{1,5},{5,1},{2,6},{6,2},{3,7},{7,3},{8,12},{12,8},{9,1... | collective-permute-start | bytes 3145736 | tf_op jit(solution)/shard_map/ppermute | solution.py:141
  333.2 53.0 %collective-permute-start.1 = (bf16[4,128,1024]{2,1,0:T(8,128)(2,1)S(1)}, bf16[4,128,1024]{2,1,0:T(8,128)(2,1)S(1)}, u32[]{:S(2)}, u32[]{:S(2)}) collective-permute-start(bf16[4,128,1024]{2,1,0:T(8,128)(2,1)S(1)} %broadcast_select_fusion.10), channel_id=1, source_target_pairs={{0,4},{4,0},{1,5},{5,1},{2,6},{6,2},{3,7},{7,3},{8,12},{12,8},{9,1... | collective-permute-start | bytes 3145736 | tf_op jit(solution)/shard_map/ppermute | solution.py:141
  408.6 27.0 %copy-start.7 = (bf16[16,128,1024]{2,1,0:T(8,128)(2,1)S(1)}, bf16[16,128,1024]{2,1,0:T(8,128)(2,1)}, u32[]{:S(2)}) copy-start(bf16[16,128,1024]{2,1,0:T(8,128)(2,1)} %pad_maximum_fusion.2) | copy-start | bytes 12582916
  433.6 2.0 copy-start
  441.3 172.2 %all-reduce.2.cloned.1.call-start = ((), (), s32[]{:S(2)}) async-start(), calls=%async_computation.10 | async-start | bytes 2097152 | tf_op jit(solution)/shard_map/psum | solution.py:228
  441.3 70.4 %copy-start.1 = (bf16[16,128,1024]{2,1,0:T(8,128)(2,1)S(1)}, bf16[16,128,1024]{2,1,0:T(8,128)(2,1)}, u32[]{:S(2)}) copy-start(bf16[16,128,1024]{2,1,0:T(8,128)(2,1)} %copy-done) | copy-start | bytes 12582916
  443.9 67.8 %collective-permute-start.3 = (bf16[8,128,1024]{2,1,0:T(8,128)(2,1)S(1)}, bf16[8,128,1024]{2,1,0:T(8,128)(2,1)S(1)}, u32[]{:S(2)}, u32[]{:S(2)}) collective-permute-start(bf16[8,128,1024]{2,1,0:T(8,128)(2,1)S(1)} %broadcast_select_fusion.2), channel_id=1, source_target_pairs={{0,4},{4,0},{1,5},{5,1},{2,6},{6,2},{3,7},{7,3},{8,12},{12,8},{9,1... | collective-permute-start | bytes 6291464 | tf_op jit(solution)/shard_map/ppermute | solution.py:141
  512.2 2.2 copy-start.5
  512.2 2.9 copy-start.13
  519.4 5.3 copy-start.8
Sparse Core Ops, SparseCore 0:
  9.5 83.0 all-gather.4
  94.2 33.1 all-gather.6
  128.9 80.3 all-gather.8
  274.0 56.2 all-gather.10
  441.4 55.5 reduce-scatter.1
  519.5 93.9 all-reduce.1
